TPU v7x, 128 devices: a whole 4x4x4 slice. The times are simulated.
128 devices in a mesh: node: 32 (over y, x, z_lo), local: 4 (over z_hi, core).
Axes of the slice: x: 4, y: 4, z: 4 (z_hi: 2, z_lo: 2; z = z_hi * 2 + z_lo), core: 2. Of those that a mesh axis runs over, the one named last changes fastest.
Arguments:
- tokens: bfloat16 [16384, 4096], P(('node', 'local')), may hold values from -6 to 6
- grad_out: bfloat16 [16384, 4096], P(('node', 'local')), may hold values from -6 to 6
- router_logits: float32 [16384, 128], P(('node', 'local')), may hold values from -20 to 280
- group_id: int32 [16384], P(('node', 'local')), may hold values from 0 to 15, as said below
- expert_ids: int32 [16384, 2], P(('node', 'local')), may hold values from 0 to 7, as said below
- w_gate: bfloat16 [32, 4096, 1536], P('node', None, 'local'), may hold values from -0.09375 to 0.09375
- w_up: bfloat16 [32, 4096, 1536], P('node', None, 'local'), may hold values from -0.09375 to 0.09375
- w_down: bfloat16 [32, 1536, 4096], P('node', 'local'), may hold values from -0.15625 to 0.15625
Outputs:
- mixed: bfloat16 [16384, 4096], P(('node', 'local'))
- d_tokens: bfloat16 [16384, 4096], P(('node', 'local'))
- d_logits: float32 [16384, 128], P(('node', 'local'))
- grad_gate: bfloat16 [32, 4096, 1536], P('node', None, 'local')
- grad_up: bfloat16 [32, 4096, 1536], P('node', None, 'local')
- grad_down: bfloat16 [32, 1536, 4096], P('node', 'local')
Inputs may be any that keep to these rules, and one draw needn't show every extreme that they name: `group_id`: A token is computed here when its group is below 4. Among the tokens of one device no expert of those groups is named by more than 6 tokens, and one such expert is named by exactly 6 tokens of every device. `expert_ids`: the two numbers of a token differ; both name experts of the token's group.
All inputs are finite; a program needn't handle non-finite values.
Results may differ from a plain program's by a relative error of at most 0.0065.
Values may be sent and summed in bfloat16 or wider, within the bound.
No kernel may reach another device: no remote copies, remote signals or barrier semaphores. Data moves between devices by JAX's collectives and lax.ppermute only.
A program may use at most 192 MiB of HBM per device.

v0:
```python
import jax
import jax.numpy as jnp
from jax import lax
from jax.sharding import PartitionSpec as P

GSIZE = 8
CAP = 6


def cut_along(value, dim, length):
    lengths = value.shape
    pieces = value.reshape(*lengths[:dim], length, lengths[dim] // length, *lengths[dim + 1 :])
    return jnp.moveaxis(pieces, dim, 0)


def piece_ends(length, count):
    unit = 8 if length >= 8 * count else 1
    return [length // unit * k // count * unit for k in range(1, count)]


def in_order(pieces, dim):
    pieces = jnp.moveaxis(pieces, 0, dim)
    lengths = pieces.shape
    return pieces.reshape(*lengths[:dim], lengths[dim] * lengths[dim + 1], *lengths[dim + 2 :])


def exchange_in_pieces(value, axis, pieces, split_dim, concat_dim):
    blocks = cut_along(value, split_dim, lax.axis_size(axis))
    cut = max(range(1, max(2, blocks.ndim - 1)), key=lambda d: blocks.shape[d])
    outs = []
    for piece in jnp.split(blocks, piece_ends(blocks.shape[cut], pieces), axis=cut):
        if piece.size:
            outs.append(lax.all_to_all(piece, axis, split_axis=0, concat_axis=0, tiled=True))
    return in_order(jnp.concatenate(outs, axis=cut), concat_dim)


def gate_weights(logits, group_ids, chosen, inside):
    probabilities = jax.nn.softmax(logits, axis=-1)
    columns = jnp.arange(logits.shape[1], dtype=jnp.int32)
    member = ((columns // GSIZE)[None, :] == group_ids[:, None]).astype(logits.dtype)
    group_mass = jnp.sum(probabilities * member, axis=1)
    picked = jnp.sum(
        jnp.where(chosen[:, :, None] == columns[None, None, :], logits[:, None, :], 0.0), axis=2
    )
    pair_share = jax.nn.softmax(picked, axis=-1)
    return jnp.where(inside[:, None], group_mass[:, None] * pair_share, 0.0)


def spread(buffer):
    arrived = lax.all_to_all(buffer, "node", split_axis=0, concat_axis=2, tiled=True)
    arrived = lax.all_gather(arrived, "local", axis=2, tiled=True)
    return arrived[0]


def collect(partial_sums):
    summed = lax.psum_scatter(partial_sums[None], "local", scatter_dimension=2, tiled=True)
    result = exchange_in_pieces(summed.astype(jnp.bfloat16), "node", 2, 2, 0)
    return result.reshape(-1, result.shape[-1])


def body(tokens, grad_out, router_logits, group_id, expert_ids, w_gate, w_up, w_down):
    owned_count = w_gate.shape[0]
    node_count = lax.axis_size("node")
    expert_total = owned_count * node_count
    window_groups = expert_total // GSIZE
    model_width = tokens.shape[1]
    inside = group_id < window_groups
    chosen = group_id[:, None] * GSIZE + expert_ids
    target = jnp.where(inside[:, None], chosen, expert_total)
    expert_range = jnp.arange(expert_total, dtype=jnp.int32)
    onehot = (target[:, :, None] == expert_range[None, None, :]).astype(jnp.int32)
    per_token = jnp.sum(onehot, axis=1)
    earlier = jnp.cumsum(per_token, axis=0) - per_token
    slot_rank = jnp.sum(onehot * earlier[:, None, :], axis=2)
    slot_index = jnp.where(inside[:, None], target * CAP + slot_rank, -1)
    slot_range = jnp.arange(expert_total * CAP, dtype=jnp.int32)
    first_pick = (slot_range[:, None] == slot_index[None, :, 0]).astype(jnp.bfloat16)
    second_pick = (slot_range[:, None] == slot_index[None, :, 1]).astype(jnp.bfloat16)
    mix_weights, pull_back = jax.vjp(
        lambda values: gate_weights(values, group_id, chosen, inside), router_logits
    )
    grad_f32 = grad_out.astype(jnp.float32)
    first_grad = (mix_weights[:, 0:1] * grad_f32).astype(jnp.bfloat16)
    second_grad = (mix_weights[:, 1:2] * grad_f32).astype(jnp.bfloat16)
    send_rows = (
        jnp.dot(first_pick, tokens, preferred_element_type=jnp.float32)
        + jnp.dot(second_pick, tokens, preferred_element_type=jnp.float32)
    ).astype(jnp.bfloat16)
    send_grads = (
        jnp.dot(first_pick, first_grad, preferred_element_type=jnp.float32)
        + jnp.dot(second_pick, second_grad, preferred_element_type=jnp.float32)
    ).astype(jnp.bfloat16)
    buffer_shape = (node_count, owned_count, CAP, model_width)
    rows_in = spread(send_rows.reshape(buffer_shape))
    gate_pre = jnp.einsum("erd,edf->erf", rows_in, w_gate, preferred_element_type=jnp.float32)
    up_pre = jnp.einsum("erd,edf->erf", rows_in, w_up, preferred_element_type=jnp.float32)
    sigmoid_gate = jax.nn.sigmoid(gate_pre)
    activated = gate_pre * sigmoid_gate
    hidden = (activated * up_pre).astype(jnp.bfloat16)
    partial_out = jnp.einsum("erf,efd->erd", hidden, w_down, preferred_element_type=jnp.float32)
    out_flat = collect(partial_out)
    grads_in = spread(send_grads.reshape(buffer_shape))
    grad_hidden = jnp.einsum("erd,efd->erf", grads_in, w_down, preferred_element_type=jnp.float32)
    grad_gate_pre = (
        grad_hidden * up_pre * sigmoid_gate * (1.0 + gate_pre * (1.0 - sigmoid_gate))
    ).astype(jnp.bfloat16)
    grad_up_pre = (grad_hidden * activated).astype(jnp.bfloat16)
    partial_in = jnp.einsum(
        "erf,edf->erd", grad_gate_pre, w_gate, preferred_element_type=jnp.float32
    ) + jnp.einsum("erf,edf->erd", grad_up_pre, w_up, preferred_element_type=jnp.float32)
    back_flat = collect(partial_in)
    grad_gate = jnp.einsum(
        "erd,erf->edf", rows_in, grad_gate_pre, preferred_element_type=jnp.float32
    ).astype(jnp.bfloat16)
    grad_up = jnp.einsum(
        "erd,erf->edf", rows_in, grad_up_pre, preferred_element_type=jnp.float32
    ).astype(jnp.bfloat16)
    grad_down = jnp.einsum(
        "erf,erd->efd", hidden, grads_in, preferred_element_type=jnp.float32
    ).astype(jnp.bfloat16)
    first_out = jnp.einsum("st,sd->td", first_pick, out_flat, preferred_element_type=jnp.float32)
    second_out = jnp.einsum("st,sd->td", second_pick, out_flat, preferred_element_type=jnp.float32)
    first_back = jnp.einsum("st,sd->td", first_pick, back_flat, preferred_element_type=jnp.float32)
    second_back = jnp.einsum(
        "st,sd->td", second_pick, back_flat, preferred_element_type=jnp.float32
    )
    mixed = (mix_weights[:, 0:1] * first_out + mix_weights[:, 1:2] * second_out).astype(
        jnp.bfloat16
    )
    d_tokens = (first_back + second_back).astype(jnp.bfloat16)
    scores = jnp.stack(
        [jnp.sum(grad_f32 * first_out, axis=1), jnp.sum(grad_f32 * second_out, axis=1)], axis=1
    )
    d_logits = pull_back(scores)[0]
    return (mixed, d_tokens, d_logits, grad_gate, grad_up, grad_down)


def solution(mesh):
    return jax.shard_map(
        body,
        mesh=mesh,
        in_specs=(
            P(("node", "local"), None),
            P(("node", "local"), None),
            P(("node", "local"), None),
            P(("node", "local")),
            P(("node", "local"), None),
            P("node", None, "local"),
            P("node", None, "local"),
            P("node", "local", None),
        ),
        out_specs=(
            P(("node", "local"), None),
            P(("node", "local"), None),
            P(("node", "local"), None),
            P("node", None, "local"),
            P("node", None, "local"),
            P("node", "local", None),
        ),
        check_vma=False,
    )
```

profile of v0, /device:TPU:0, one launch (start us, length us, event | category | flops | bytes accessed | tf_op | source)
XLA Modules:
  0.0 582.0 jit_solution(17738413348024515923)
XLA Ops:
  17.0 37.9 %all_to_all.44 = bf16[32,1,6,4096]{3,2,1,0:T(8,128)(2,1)} all-to-all(bf16[32,1,6,4096]{3,2,1,0:T(8,128)(2,1)} %bitcast.95), channel_id=1, replica_groups=mesh['node'=32,'local'=4] {'node'}, dimensions={0} | all-to-all | bytes 3145728 | tf_op jit(solution)/shard_map/all_to_all | solution.py:50
  58.7 48.7 %all-gather.3.cloned.1.call-done = bf16[1,1,768,4096]{3,2,1,0:T(8,128)(2,1)} async-done(((bf16[1,1,192,4096]{3,2,1,0:T(8,128)(2,1)}), bf16[1,1,768,4096]{3,2,1,0:T(8,128)(2,1)}) %all-gather.3.cloned.1.call-update) | async-done | bytes 6291472 | tf_op jit(solution)/shard_map/all_gather | solution.py:51
  107.4 6.6 %fusion.10 = f32[768,384]{1,0:T(8,128)S(1)} fusion(bf16[1,1,768,4096]{3,2,1,0:T(8,128)(2,1)} %all-gather.3.cloned.1.call-done, bf16[1,4096,384]{2,1,0:T(8,128)(2,1)} %param.13), kind=kOutput, calls=%fused_computation.12 | convolution fusion | flops 2415919104 | bytes 10616832 | tf_op jit(solution)/shard_map/erd,edf->erf/dot_general | solution.py:95
  114.0 4.5 multiply_convert_fusion.2
  119.3 6.4 %convolution_bitcast_fusion = f32[1,1,768,4096]{3,2,1,0:T(8,128)} fusion(bf16[768,384]{1,0:T(8,128)(2,1)S(1)} %get-tuple-element.26, bf16[1,384,4096]{2,1,0:T(8,128)(2,1)S(1)} %copy-done), kind=kOutput, calls=%fused_computation.1 | convolution fusion | flops 2415919104 | bytes 16318464 | tf_op jit(solution)/shard_map/erf,efd->erd/dot_general | solution.py:100
  125.8 105.4 %reduce-scatter.3.cloned.1.call-done = f32[1,1,192,4096]{3,2,1,0:T(8,128)} async-done(((f32[1,1,768,4096]{3,2,1,0:T(8,128)}), f32[1,1,192,4096]{3,2,1,0:T(8,128)}) %reduce-scatter.3.cloned.1.call-update) | async-done | bytes 3145744 | tf_op jit(solution)/shard_map/reduce_scatter | solution.py:56
  237.9 4.7 slice_bitcast_fusion.3
  242.6 7.4 %all-to-all-start.1 = ((bf16[32,1,1,3,4096]{4,3,2,1,0:T(4,128)(2,1)}), bf16[32,1,1,3,4096]{4,3,2,1,0:T(4,128)(2,1)}, u32[]{:S(2)}, u32[]{:S(2)}) async-start(bf16[32,1,1,3,4096]{4,3,2,1,0:T(4,128)(2,1)} %get-tuple-element.18), calls=%async_computation.2 | async-start | bytes 2097152 | tf_op jit(solution)/shard_map/all_to_all | solution.py:33
  250.4 17.5 %all-to-all-done.1 = bf16[32,1,1,3,4096]{4,3,2,1,0:T(4,128)(2,1)} async-done(((bf16[32,1,1,3,4096]{4,3,2,1,0:T(4,128)(2,1)}), bf16[32,1,1,3,4096]{4,3,2,1,0:T(4,128)(2,1)}, u32[]{:S(2)}, u32[]{:S(2)}) %all-to-all-start.1) | async-done | bytes 786464 | tf_op jit(solution)/shard_map/all_to_all | solution.py:33
  267.9 4.7 all-to-all-start.2
  272.6 10.2 %all-gather.5.cloned.1.call-start = ((), (), s32[]{:S(2)}) async-start(), calls=%async_computation.10 | async-start | bytes 7864320 | tf_op jit(solution)/shard_map/all_gather | solution.py:51
  283.0 6.4 %all-to-all-done.2 = bf16[32,1,1,3,4096]{4,3,2,1,0:T(4,128)(2,1)} async-done(((bf16[32,1,1,3,4096]{4,3,2,1,0:T(4,128)(2,1)}), bf16[32,1,1,3,4096]{4,3,2,1,0:T(4,128)(2,1)}, u32[]{:S(2)}, u32[]{:S(2)}) %all-to-all-start.2) | async-done | bytes 786464 | tf_op jit(solution)/shard_map/all_to_all | solution.py:33
  289.4 3.9 pad_maximum_fusion
  307.6 31.9 %all_to_all.45 = bf16[32,1,6,4096]{3,2,1,0:T(8,128)(2,1)} all-to-all(bf16[32,1,6,4096]{3,2,1,0:T(8,128)(2,1)} %bitcast.96), channel_id=1, replica_groups=mesh['node'=32,'local'=4] {'node'}, dimensions={0} | all-to-all | bytes 3145728 | tf_op jit(solution)/shard_map/all_to_all | solution.py:50
  343.2 47.0 %all-gather.5.cloned.1.call-done = bf16[1,1,768,4096]{3,2,1,0:T(8,128)(2,1)} async-done(((bf16[1,1,192,4096]{3,2,1,0:T(8,128)(2,1)}), bf16[1,1,768,4096]{3,2,1,0:T(8,128)(2,1)}) %all-gather.5.cloned.1.call-update) | async-done | bytes 6291472 | tf_op jit(solution)/shard_map/all_gather | solution.py:51
  390.3 7.3 %multiply_convert_fusion = (bf16[768,384]{1,0:T(8,128)(2,1)S(1)}, bf16[768,384]{1,0:T(8,128)(2,1)S(1)}) fusion(f32[768,384]{1,0:T(8,128)} %copy-done.20, f32[768,384]{1,0:T(8,128)} %get-tuple-element.27, bf16[1,384,4096]{2,1,0:T(8,128)(2,1)S(1)} %copy-done, bf16[1,1,768,4096]{3,2,1,0:T(8,128)(2,1)} %all-gather.5.cloned.1.call-done), kind=kOutput, calls=%fused_computation.44 | convolution fusion | flops 2419752960 | bytes 12976128 | tf_op jit(solution)/shard_map/erd,efd->erf/dot_general | solution.py:103
  401.1 6.5 %add_bitcast_fusion = f32[1,1,768,4096]{3,2,1,0:T(8,128)} fusion(f32[768,4096]{1,0:T(8,128)S(1)} %fusion.37, bf16[768,384]{1,0:T(8,128)(2,1)S(1)} %get-tuple-element.14, bf16[1,4096,384]{2,1,0:T(8,128)(2,1)S(1)} %copy-done.11), kind=kOutput, calls=%fused_computation | convolution fusion | flops 2419064832 | bytes 28901376 | tf_op jit(solution)/shard_map/erf,edf->erd/dot_general | solution.py:110
  412.2 100.9 %reduce-scatter.5.cloned.1.call-done = f32[1,1,192,4096]{3,2,1,0:T(8,128)} async-done(((f32[1,1,768,4096]{3,2,1,0:T(8,128)}), f32[1,1,192,4096]{3,2,1,0:T(8,128)}) %reduce-scatter.5.cloned.1.call-update) | async-done | bytes 3145744 | tf_op jit(solution)/shard_map/reduce_scatter | solution.py:56
  521.2 7.5 %all-to-all-start.4 = ((bf16[32,1,1,3,4096]{4,3,2,1,0:T(4,128)(2,1)}), bf16[32,1,1,3,4096]{4,3,2,1,0:T(4,128)(2,1)S(1)}, u32[]{:S(2)}, u32[]{:S(2)}) async-start(bf16[32,1,1,3,4096]{4,3,2,1,0:T(4,128)(2,1)} %get-tuple-element.16), calls=%async_computation.6 | async-start | bytes 2097152 | tf_op jit(solution)/shard_map/all_to_all | solution.py:33
  529.5 7.9 %fusion.24 = bf16[1,4096,384]{2,1,0:T(8,128)(2,1)} fusion(bf16[768,384]{1,0:T(8,128)(2,1)S(1)} %copy-done.15, bf16[1,1,768,4096]{3,2,1,0:T(8,128)(2,1)} %all-gather.3.cloned.1.call-done), kind=kOutput, calls=%fused_computation.20 | convolution fusion | flops 2417491968 | bytes 10027008 | tf_op jit(solution)/shard_map/erd,erf->edf/dot_general | solution.py:115
  537.5 8.9 %all-to-all-done.4 = bf16[32,1,1,3,4096]{4,3,2,1,0:T(4,128)(2,1)S(1)} async-done(((bf16[32,1,1,3,4096]{4,3,2,1,0:T(4,128)(2,1)}), bf16[32,1,1,3,4096]{4,3,2,1,0:T(4,128)(2,1)S(1)}, u32[]{:S(2)}, u32[]{:S(2)}) %all-to-all-start.4) | async-done | bytes 786464 | tf_op jit(solution)/shard_map/all_to_all | solution.py:33
  546.4 4.7 all-to-all-start.5
  551.1 7.2 %fusion.21 = bf16[1,384,4096]{2,1,0:T(8,128)(2,1)} fusion(bf16[768,384]{1,0:T(8,128)(2,1)S(1)} %copy-done.9, bf16[1,1,768,4096]{3,2,1,0:T(8,128)(2,1)} %all-gather.5.cloned.1.call-done), kind=kOutput, calls=%fused_computation.19 | convolution fusion | flops 2417491968 | bytes 10027008 | tf_op jit(solution)/shard_map/erf,erd->efd/dot_general | solution.py:118
  558.3 7.9 %fusion.27 = bf16[1,4096,384]{2,1,0:T(8,128)(2,1)} fusion(bf16[768,384]{1,0:T(8,128)(2,1)S(1)} %copy-done.17, bf16[1,1,768,4096]{3,2,1,0:T(8,128)(2,1)} %all-gather.3.cloned.1.call-done), kind=kOutput, calls=%fused_computation.21 | convolution fusion | flops 2417491968 | bytes 10027008 | tf_op jit(solution)/shard_map/erd,erf->edf/dot_general | solution.py:112
  (100 shorter events, 65.5 us)
Async XLA Ops:
  7.2 112.2 %copy-start = (bf16[1,384,4096]{2,1,0:T(8,128)(2,1)S(1)}, bf16[1,384,4096]{2,1,0:T(8,128)(2,1)}, u32[]{:S(2)}) copy-start(bf16[1,384,4096]{2,1,0:T(8,128)(2,1)} %param.15) | copy-start | bytes 9437188
  7.2 100.2 %all-gather.3.cloned.1.call-start = ((), (), s32[]{:S(2)}) async-start(), calls=%async_computation.8 | async-start | bytes 7864320 | tf_op jit(solution)/shard_map/all_gather | solution.py:51
  58.6 172.6 %reduce-scatter.3.cloned.1.call-start = ((), (), s32[]{:S(2)}) async-start(), calls=%async_computation.9 | async-start | bytes 15728640 | tf_op jit(solution)/shard_map/reduce_scatter | solution.py:56
  107.4 6.6 %copy-start.10 = (bf16[1,4096,384]{2,1,0:T(8,128)(2,1)S(1)}, bf16[1,4096,384]{2,1,0:T(8,128)(2,1)}, u32[]{:S(2)}) copy-start(bf16[1,4096,384]{2,1,0:T(8,128)(2,1)} %param.14) | copy-start | bytes 9437188
  107.4 6.6 %copy-start.19 = (bf16[1,1,768,4096]{3,2,1,0:T(8,128)(2,1)S(1)}, bf16[1,1,768,4096]{3,2,1,0:T(8,128)(2,1)}, u32[]{:S(2)}) copy-start(bf16[1,1,768,4096]{3,2,1,0:T(8,128)(2,1)} %all-gather.3.cloned.1.call-done) | copy-start | bytes 18874372
  114.0 4.5 copy-start.20
  242.6 7.5 %copy-start.13 = (f32[128,128]{1,0:T(8,128)S(1)}, f32[128,128]{1,0:T(8,128)}, u32[]{:S(2)}) copy-start(f32[128,128]{1,0:T(8,128)} %param.10) | copy-start | bytes 196612
  242.6 25.3 %all-to-all-start.1 = ((bf16[32,1,1,3,4096]{4,3,2,1,0:T(4,128)(2,1)}), bf16[32,1,1,3,4096]{4,3,2,1,0:T(4,128)(2,1)}, u32[]{:S(2)}, u32[]{:S(2)}) async-start(bf16[32,1,1,3,4096]{4,3,2,1,0:T(4,128)(2,1)} %get-tuple-element.18), calls=%async_computation.2 | async-start | bytes 2097152 | tf_op jit(solution)/shard_map/all_to_all | solution.py:33
  267.9 21.5 %all-to-all-start.2 = ((bf16[32,1,1,3,4096]{4,3,2,1,0:T(4,128)(2,1)}), bf16[32,1,1,3,4096]{4,3,2,1,0:T(4,128)(2,1)}, u32[]{:S(2)}, u32[]{:S(2)}) async-start(bf16[32,1,1,3,4096]{4,3,2,1,0:T(4,128)(2,1)} %get-tuple-element.19), calls=%async_computation.3 | async-start | bytes 2097152 | tf_op jit(solution)/shard_map/all_to_all | solution.py:33
  272.6 117.7 %all-gather.5.cloned.1.call-start = ((), (), s32[]{:S(2)}) async-start(), calls=%async_computation.10 | async-start | bytes 7864320 | tf_op jit(solution)/shard_map/all_gather | solution.py:51
  297.0 2.2 copy-start.6
  299.1 2.2 copy-start.2
  299.1 2.2 copy-start.18
  343.2 169.9 %reduce-scatter.5.cloned.1.call-start = ((), (), s32[]{:S(2)}) async-start(), calls=%async_computation.11 | async-start | bytes 15728640 | tf_op jit(solution)/shard_map/reduce_scatter | solution.py:56
  390.3 7.3 %copy-start.12 = (bf16[1,4096,384]{2,1,0:T(8,128)(2,1)S(1)}, bf16[1,4096,384]{2,1,0:T(8,128)(2,1)}, u32[]{:S(2)}) copy-start(bf16[1,4096,384]{2,1,0:T(8,128)(2,1)} %param.13) | copy-start | bytes 9437188
  397.6 3.5 copy-start.16
  397.6 3.5 copy-start.14
  397.6 3.5 copy-start.11
  521.2 8.3 %copy-start.15 = (bf16[768,384]{1,0:T(8,128)(2,1)S(1)}, bf16[768,384]{1,0:T(8,128)(2,1)}, u32[]{:S(2)}) copy-start(bf16[768,384]{1,0:T(8,128)(2,1)} %copy-done.14) | copy-start | bytes 1769476
  521.2 25.2 %all-to-all-start.4 = ((bf16[32,1,1,3,4096]{4,3,2,1,0:T(4,128)(2,1)}), bf16[32,1,1,3,4096]{4,3,2,1,0:T(4,128)(2,1)S(1)}, u32[]{:S(2)}, u32[]{:S(2)}) async-start(bf16[32,1,1,3,4096]{4,3,2,1,0:T(4,128)(2,1)} %get-tuple-element.16), calls=%async_computation.6 | async-start | bytes 2097152 | tf_op jit(solution)/shard_map/all_to_all | solution.py:33
  537.5 13.6 %copy-start.9 = (bf16[768,384]{1,0:T(8,128)(2,1)S(1)}, bf16[768,384]{1,0:T(8,128)(2,1)}, u32[]{:S(2)}) copy-start(bf16[768,384]{1,0:T(8,128)(2,1)} %copy-done.8) | copy-start | bytes 1769476
  546.4 21.5 %all-to-all-start.5 = ((bf16[32,1,1,3,4096]{4,3,2,1,0:T(4,128)(2,1)}), bf16[32,1,1,3,4096]{4,3,2,1,0:T(4,128)(2,1)}, u32[]{:S(2)}, u32[]{:S(2)}) async-start(bf16[32,1,1,3,4096]{4,3,2,1,0:T(4,128)(2,1)} %get-tuple-element.17), calls=%async_computation.7 | async-start | bytes 2097152 | tf_op jit(solution)/shard_map/all_to_all | solution.py:33
  551.1 7.2 %copy-start.17 = (bf16[768,384]{1,0:T(8,128)(2,1)S(1)}, bf16[768,384]{1,0:T(8,128)(2,1)}, u32[]{:S(2)}) copy-start(bf16[768,384]{1,0:T(8,128)(2,1)} %copy-done.16) | copy-start | bytes 1769476
  571.6 3.5 copy-start.1
  (5 other events, 8.4 us)
Sparse Core Ops, SparseCore 0:
  58.7 48.6 all-gather.2
  125.9 105.2 reduce-scatter.2
  343.3 46.9 all-gather.4
  407.7 105.3 reduce-scatter.4
where the time goes:
time: 591 us; the launch traced here: 582 us
  waiting for transfers between devices  337 us (57%)
  matrix products  71.5 us (12%)
  blocking collectives  69.8 us (12%)
  local copies, waits for them, and re-layouts  35.1 us (6%)
  starting transfers between devices  34.6 us (6%)
  other arithmetic  19.9 us (3%)
  between operations  14.5 us (2%)
    reduce_scatter x2, waiting for transfers between devices, collect(): lax.psum_scatter(partial_sums[None], 'local', scatter_dimension=2, tiled=...  206 us
    all_gather x2, waiting for transfers between devices, spread(): arrived = lax.all_gather(arrived, 'local', axis=2, tiled=True)  95.8 us
    all_to_all x2, blocking collectives, spread(): lax.all_to_all(buffer, 'node', split_axis=0, concat_axis=2, tiled=True)  69.8 us
    all_to_all x4, waiting for transfers between devices, exchange_in_pieces(): lax.all_to_all(piece, axis, split_axis=0, concat_axis=0, tiled=True)  34.5 us
    all_to_all x4, starting transfers between devices, exchange_in_pieces(): lax.all_to_all(piece, axis, split_axis=0, concat_axis=0, tiled=True)  24.3 us
  transfers between devices with their start and end apart: 8, of which 8 were waited for; matrix products, arithmetic and copies ran while one was open for 5% of the time, Pallas kernels for 0%

commit v1 on v0

--- a/solution.py
+++ b/solution.py
@@ -5,6 +5,11 @@
 
 GSIZE = 8
 CAP = 6
+
+
+def all_by_exchange(x, name, dim):
+    stack = jnp.stack([x] * lax.axis_size(name))
+    return jnp.concatenate(lax.all_to_all(stack, name, 0, 0), axis=dim)
 
 
 def cut_along(value, dim, length):
@@ -48,7 +53,7 @@
 
 def spread(buffer):
     arrived = lax.all_to_all(buffer, "node", split_axis=0, concat_axis=2, tiled=True)
-    arrived = lax.all_gather(arrived, "local", axis=2, tiled=True)
+    arrived = all_by_exchange(arrived, "local", 2)
     return arrived[0]
 
 

time: 591 us -> 650 us (1.100)
  blocking collectives: 69.8 us -> 222 us
  waiting for transfers between devices: 337 us -> 243 us
  matrix products: 71.5 us -> 64.7 us
    all_to_all x0 -> x2, blocking collectives: none -> 152 us  [all_by_exchange(): return jnp.concatenate(lax.all_to_all(stack, name, 0, 0), axis=dim)]
    all_gather x2 -> x0, waiting for transfers between devices: 95.8 us -> none  [spread(): arrived = lax.all_gather(arrived, 'local', axis=2, tiled=True)]
    another operation x0 -> x4, local copies, waits for them, and re-layouts: none -> 11.7 us  [all_by_exchange(): stack = jnp.stack([x] * lax.axis_size(name))]
    all_to_all x4, starting transfers between devices: 24.3 us -> 34.8 us  [exchange_in_pieces(): lax.all_to_all(piece, axis, split_axis=0, concat_axis=0, tiled=True)]
    all_gather x2 -> x0, starting transfers between devices: 10.2 us -> none  [spread(): arrived = lax.all_gather(arrived, 'local', axis=2, tiled=True)]
    all_to_all x4, waiting for transfers between devices: 34.5 us -> 44.6 us  [exchange_in_pieces(): lax.all_to_all(piece, axis, split_axis=0, concat_axis=0, tiled=True)]
    reduce_scatter x2, waiting for transfers between devices: 206 us -> 198 us  [collect(): lax.psum_scatter(partial_sums[None], 'local', scatter_dimension=2, tiled=...]
    all_to_all x2 -> x0, local copies, waits for them, and re-layouts: 7.32 us -> none  [spread(): lax.all_to_all(buffer, 'node', split_axis=0, concat_axis=2, tiled=True)]
  transfers between devices with their start and end apart: 8 -> 6, of which waited for: 8 -> 6; matrix products, arithmetic and copies ran while one was open for 5% -> 4% of each run, Pallas kernels for 0% -> 0%
where the time goes in v1:
time: 650 us; the launch traced here: 640 us
  waiting for transfers between devices  243 us (37%)
  blocking collectives  222 us (34%)
  matrix products  64.7 us (10%)
  local copies, waits for them, and re-layouts  40.6 us (6%)
  starting transfers between devices  34.9 us (5%)
  other arithmetic  19.9 us (3%)
  between operations  14.8 us (2%)
    reduce_scatter x2, waiting for transfers between devices, collect(): lax.psum_scatter(partial_sums[None], 'local', scatter_dimension=2, tiled=...  198 us
    all_to_all x2, blocking collectives, all_by_exchange(): return jnp.concatenate(lax.all_to_all(stack, name, 0, 0), axis=dim)  152 us
    all_to_all x2, blocking collectives, spread(): lax.all_to_all(buffer, 'node', split_axis=0, concat_axis=2, tiled=True)  69.8 us
    all_to_all x4, waiting for transfers between devices, exchange_in_pieces(): lax.all_to_all(piece, axis, split_axis=0, concat_axis=0, tiled=True)  44.6 us
    all_to_all x4, starting transfers between devices, exchange_in_pieces(): lax.all_to_all(piece, axis, split_axis=0, concat_axis=0, tiled=True)  34.8 us
  transfers between devices with their start and end apart: 6, of which 6 were waited for; matrix products, arithmetic and copies ran while one was open for 4% of the time, Pallas kernels for 0%

profile of v1, /device:TPU:0, one launch (start us, length us, event | category | flops | bytes accessed | tf_op | source)
XLA Modules:
  0.0 639.6 jit_solution(6252686141998231283)
XLA Ops:
  17.0 37.9 %all_to_all.48 = bf16[32,1,6,4096]{3,2,1,0:T(8,128)(2,1)} all-to-all(bf16[32,1,6,4096]{3,2,1,0:T(8,128)(2,1)} %bitcast.75), channel_id=1, replica_groups=mesh['node'=32,'local'=4] {'node'}, dimensions={0} | all-to-all | bytes 3145728 | tf_op jit(solution)/shard_map/all_to_all | solution.py:55
  54.9 3.7 stack.27
  60.8 77.1 %all_to_all.49 = bf16[4,1,1,192,4096]{4,3,2,1,0:T(8,128)(2,1)S(1)} all-to-all(bf16[4,1,1,192,4096]{4,3,2,1,0:T(8,128)(2,1)S(1)} %stack.28), channel_id=1, replica_groups=mesh['node'=32,'local'=4] {'local'}, dimensions={0} | all-to-all | bytes 12582912 | tf_op jit(solution)/shard_map/all_to_all | solution.py:12
  142.0 4.5 multiply_convert_fusion.2
  147.3 6.3 convolution_bitcast_fusion
  153.7 101.3 %reduce-scatter.3.cloned.1.call-done = f32[1,1,192,4096]{3,2,1,0:T(8,128)} async-done(((f32[1,1,768,4096]{3,2,1,0:T(8,128)}), f32[1,1,192,4096]{3,2,1,0:T(8,128)}) %reduce-scatter.3.cloned.1.call-update) | async-done | bytes 3145744 | tf_op jit(solution)/shard_map/reduce_scatter | solution.py:61
  261.8 4.7 slice_bitcast_fusion.3
  266.5 7.4 %all-to-all-start.2 = ((bf16[32,1,1,3,4096]{4,3,2,1,0:T(4,128)(2,1)}), bf16[32,1,1,3,4096]{4,3,2,1,0:T(4,128)(2,1)}, u32[]{:S(2)}, u32[]{:S(2)}) async-start(bf16[32,1,1,3,4096]{4,3,2,1,0:T(4,128)(2,1)} %get-tuple-element.18), calls=%async_computation.3 | async-start | bytes 2097152 | tf_op jit(solution)/shard_map/all_to_all | solution.py:38
  274.2 17.5 %all-to-all-done.2 = bf16[32,1,1,3,4096]{4,3,2,1,0:T(4,128)(2,1)} async-done(((bf16[32,1,1,3,4096]{4,3,2,1,0:T(4,128)(2,1)}), bf16[32,1,1,3,4096]{4,3,2,1,0:T(4,128)(2,1)}, u32[]{:S(2)}, u32[]{:S(2)}) %all-to-all-start.2) | async-done | bytes 786464 | tf_op jit(solution)/shard_map/all_to_all | solution.py:38
  291.7 15.2 %all-to-all-start.3 = ((bf16[32,1,1,3,4096]{4,3,2,1,0:T(4,128)(2,1)}), bf16[32,1,1,3,4096]{4,3,2,1,0:T(4,128)(2,1)}, u32[]{:S(2)}, u32[]{:S(2)}) async-start(bf16[32,1,1,3,4096]{4,3,2,1,0:T(4,128)(2,1)} %get-tuple-element.19), calls=%async_computation.4 | async-start | bytes 2097152 | tf_op jit(solution)/shard_map/all_to_all | solution.py:38
  307.2 16.5 %all-to-all-done.3 = bf16[32,1,1,3,4096]{4,3,2,1,0:T(4,128)(2,1)} async-done(((bf16[32,1,1,3,4096]{4,3,2,1,0:T(4,128)(2,1)}), bf16[32,1,1,3,4096]{4,3,2,1,0:T(4,128)(2,1)}, u32[]{:S(2)}, u32[]{:S(2)}) %all-to-all-start.3) | async-done | bytes 786464 | tf_op jit(solution)/shard_map/all_to_all | solution.py:38
  323.7 3.9 pad_maximum_fusion
  341.9 31.9 %all_to_all.50 = bf16[32,1,6,4096]{3,2,1,0:T(8,128)(2,1)} all-to-all(bf16[32,1,6,4096]{3,2,1,0:T(8,128)(2,1)} %bitcast.76), channel_id=1, replica_groups=mesh['node'=32,'local'=4] {'node'}, dimensions={0} | all-to-all | bytes 3145728 | tf_op jit(solution)/shard_map/all_to_all | solution.py:55
  373.8 3.7 stack.29
  379.7 75.2 %all_to_all.51 = bf16[4,1,1,192,4096]{4,3,2,1,0:T(8,128)(2,1)S(1)} all-to-all(bf16[4,1,1,192,4096]{4,3,2,1,0:T(8,128)(2,1)S(1)} %stack.30), channel_id=1, replica_groups=mesh['node'=32,'local'=4] {'local'}, dimensions={0} | all-to-all | bytes 12582912 | tf_op jit(solution)/shard_map/all_to_all | solution.py:12
  454.9 3.8 multiply_convert_fusion
  462.6 6.4 %add_bitcast_fusion = f32[1,1,768,4096]{3,2,1,0:T(8,128)} fusion(f32[768,4096]{1,0:T(8,128)S(1)} %fusion.12, bf16[768,384]{1,0:T(8,128)(2,1)S(1)} %get-tuple-element.14, bf16[1,4096,384]{2,1,0:T(8,128)(2,1)S(1)} %copy-done.13), kind=kOutput, calls=%fused_computation | convolution fusion | flops 2419064832 | bytes 28901376 | tf_op jit(solution)/shard_map/erf,edf->erd/dot_general | solution.py:115
  473.6 96.8 %reduce-scatter.5.cloned.1.call-done = f32[1,1,192,4096]{3,2,1,0:T(8,128)} async-done(((f32[1,1,768,4096]{3,2,1,0:T(8,128)}), f32[1,1,192,4096]{3,2,1,0:T(8,128)}) %reduce-scatter.5.cloned.1.call-update) | async-done | bytes 3145744 | tf_op jit(solution)/shard_map/reduce_scatter | solution.py:61
  578.5 7.5 %all-to-all-start.6 = ((bf16[32,1,1,3,4096]{4,3,2,1,0:T(4,128)(2,1)}), bf16[32,1,1,3,4096]{4,3,2,1,0:T(4,128)(2,1)S(1)}, u32[]{:S(2)}, u32[]{:S(2)}) async-start(bf16[32,1,1,3,4096]{4,3,2,1,0:T(4,128)(2,1)} %get-tuple-element.16), calls=%async_computation.8 | async-start | bytes 2097152 | tf_op jit(solution)/shard_map/all_to_all | solution.py:38
  586.8 7.9 %fusion.1 = bf16[1,4096,384]{2,1,0:T(8,128)(2,1)} fusion(bf16[768,4096]{1,0:T(8,128)(2,1)} %bitcast.79, bf16[768,384]{1,0:T(8,128)(2,1)S(1)} %copy-done.18), kind=kOutput, calls=%fused_computation.8 | convolution fusion | flops 2417491968 | bytes 10027008 | tf_op jit(solution)/shard_map/erd,erf->edf/dot_general | solution.py:120
  594.7 8.9 %all-to-all-done.6 = bf16[32,1,1,3,4096]{4,3,2,1,0:T(4,128)(2,1)S(1)} async-done(((bf16[32,1,1,3,4096]{4,3,2,1,0:T(4,128)(2,1)}), bf16[32,1,1,3,4096]{4,3,2,1,0:T(4,128)(2,1)S(1)}, u32[]{:S(2)}, u32[]{:S(2)}) %all-to-all-start.6) | async-done | bytes 786464 | tf_op jit(solution)/shard_map/all_to_all | solution.py:38
  603.7 4.7 all-to-all-start.7
  608.4 7.2 %fusion.2 = bf16[1,384,4096]{2,1,0:T(8,128)(2,1)} fusion(bf16[768,384]{1,0:T(8,128)(2,1)S(1)} %copy-done.11, bf16[768,4096]{1,0:T(8,128)(2,1)} %bitcast.74), kind=kOutput, calls=%fused_computation.9 | convolution fusion | flops 2417491968 | bytes 10027008 | tf_op jit(solution)/shard_map/erf,erd->efd/dot_general | solution.py:123
  615.5 7.9 %fusion = bf16[1,4096,384]{2,1,0:T(8,128)(2,1)} fusion(bf16[768,4096]{1,0:T(8,128)(2,1)} %bitcast.80, bf16[768,384]{1,0:T(8,128)(2,1)S(1)} %copy-done.20), kind=kOutput, calls=%fused_computation.7 | convolution fusion | flops 2417491968 | bytes 10027008 | tf_op jit(solution)/shard_map/erd,erf->edf/dot_general | solution.py:117
  (106 shorter events, 66.9 us)
Async XLA Ops:
  7.2 140.2 %copy-start = (bf16[1,384,4096]{2,1,0:T(8,128)(2,1)S(1)}, bf16[1,384,4096]{2,1,0:T(8,128)(2,1)}, u32[]{:S(2)}) copy-start(bf16[1,384,4096]{2,1,0:T(8,128)(2,1)} %param.15) | copy-start | bytes 9437188
  7.2 247.8 %reduce-scatter.3.cloned.1.call-start = ((), (), s32[]{:S(2)}) async-start(), calls=%async_computation.10 | async-start | bytes 15728640 | tf_op jit(solution)/shard_map/reduce_scatter | solution.py:61
  60.8 77.1 %copy-start.14 = (bf16[1,4096,384]{2,1,0:T(8,128)(2,1)S(1)}, bf16[1,4096,384]{2,1,0:T(8,128)(2,1)}, u32[]{:S(2)}) copy-start(bf16[1,4096,384]{2,1,0:T(8,128)(2,1)} %param.13) | copy-start | bytes 9437188
  137.8 3.4 copy-start.8
  137.8 4.2 copy-start.12
  142.0 4.5 copy-start.22
  266.5 7.5 %copy-start.16 = (f32[128,128]{1,0:T(8,128)S(1)}, f32[128,128]{1,0:T(8,128)}, u32[]{:S(2)}) copy-start(f32[128,128]{1,0:T(8,128)} %param.10) | copy-start | bytes 196612
  266.5 25.3 %all-to-all-start.2 = ((bf16[32,1,1,3,4096]{4,3,2,1,0:T(4,128)(2,1)}), bf16[32,1,1,3,4096]{4,3,2,1,0:T(4,128)(2,1)}, u32[]{:S(2)}, u32[]{:S(2)}) async-start(bf16[32,1,1,3,4096]{4,3,2,1,0:T(4,128)(2,1)} %get-tuple-element.18), calls=%async_computation.3 | async-start | bytes 2097152 | tf_op jit(solution)/shard_map/all_to_all | solution.py:38
  291.7 32.0 %all-to-all-start.3 = ((bf16[32,1,1,3,4096]{4,3,2,1,0:T(4,128)(2,1)}), bf16[32,1,1,3,4096]{4,3,2,1,0:T(4,128)(2,1)}, u32[]{:S(2)}, u32[]{:S(2)}) async-start(bf16[32,1,1,3,4096]{4,3,2,1,0:T(4,128)(2,1)} %get-tuple-element.19), calls=%async_computation.4 | async-start | bytes 2097152 | tf_op jit(solution)/shard_map/all_to_all | solution.py:38
  306.9 263.4 %reduce-scatter.5.cloned.1.call-start = ((), (), s32[]{:S(2)}) async-start(), calls=%async_computation.11 | async-start | bytes 15728640 | tf_op jit(solution)/shard_map/reduce_scatter | solution.py:61
  333.5 2.2 copy-start.21
  379.7 75.2 %copy-start.23 = (f32[768,384]{1,0:T(8,128)S(1)}, f32[768,384]{1,0:T(8,128)}, u32[]{:S(2)}) copy-start(f32[768,384]{1,0:T(8,128)} %copy-done.22) | copy-start | bytes 3538948
  379.7 75.2 %copy-start.24 = (f32[768,384]{1,0:T(8,128)S(1)}, f32[768,384]{1,0:T(8,128)}, u32[]{:S(2)}) copy-start(f32[768,384]{1,0:T(8,128)} %get-tuple-element.27) | copy-start | bytes 3538948
  454.9 3.8 copy-start.2
  454.9 4.2 copy-start.15
  458.7 3.8 copy-start.19
  458.7 3.8 copy-start.17
  459.1 3.5 copy-start.13
  578.5 8.3 %copy-start.18 = (bf16[768,384]{1,0:T(8,128)(2,1)S(1)}, bf16[768,384]{1,0:T(8,128)(2,1)}, u32[]{:S(2)}) copy-start(bf16[768,384]{1,0:T(8,128)(2,1)} %copy-done.17) | copy-start | bytes 1769476
  578.5 25.2 %all-to-all-start.6 = ((bf16[32,1,1,3,4096]{4,3,2,1,0:T(4,128)(2,1)}), bf16[32,1,1,3,4096]{4,3,2,1,0:T(4,128)(2,1)S(1)}, u32[]{:S(2)}, u32[]{:S(2)}) async-start(bf16[32,1,1,3,4096]{4,3,2,1,0:T(4,128)(2,1)} %get-tuple-element.16), calls=%async_computation.8 | async-start | bytes 2097152 | tf_op jit(solution)/shard_map/all_to_all | solution.py:38
  594.7 13.6 %copy-start.11 = (bf16[768,384]{1,0:T(8,128)(2,1)S(1)}, bf16[768,384]{1,0:T(8,128)(2,1)}, u32[]{:S(2)}) copy-start(bf16[768,384]{1,0:T(8,128)(2,1)} %copy-done.10) | copy-start | bytes 1769476
  603.7 21.5 %all-to-all-start.7 = ((bf16[32,1,1,3,4096]{4,3,2,1,0:T(4,128)(2,1)}), bf16[32,1,1,3,4096]{4,3,2,1,0:T(4,128)(2,1)}, u32[]{:S(2)}, u32[]{:S(2)}) async-start(bf16[32,1,1,3,4096]{4,3,2,1,0:T(4,128)(2,1)} %get-tuple-element.17), calls=%async_computation.9 | async-start | bytes 2097152 | tf_op jit(solution)/shard_map/all_to_all | solution.py:38
  608.3 7.2 %copy-start.20 = (bf16[768,384]{1,0:T(8,128)(2,1)S(1)}, bf16[768,384]{1,0:T(8,128)(2,1)}, u32[]{:S(2)}) copy-start(bf16[768,384]{1,0:T(8,128)(2,1)} %copy-done.19) | copy-start | bytes 1769476
  628.9 3.5 copy-start.1
  (7 other events, 12.7 us)
Sparse Core Ops, SparseCore 0:
  153.8 101.1 reduce-scatter.2
  469.1 101.1 reduce-scatter.4
